TPU v7x, 32 devices: a whole 2x2x4 slice. The times are simulated.
32 devices in a mesh: freq: 4 (over x, core), tile: 8 (over z, y).
Axes of the slice: x: 2, y: 2, z: 4, core: 2. Of those that a mesh axis runs over, the one named last changes fastest.
Arguments:
- model_field: bfloat16 [4, 4096, 256], P('freq', 'tile'), may hold values from -6 to 6
- data_field: bfloat16 [4, 4096, 256], P('freq', 'tile'), may hold values from -6 to 6
- u_codes: bfloat16 [4, 2, 4096, 704], P('freq', None, 'tile'), may hold values from -128 to 127, as said below
- u_scales: float32 [4, 8, 704], P('freq', 'tile'), as said below
- v_codes: bfloat16 [4, 2, 4096, 704], P('freq', None, 'tile'), may hold values from -128 to 127, as said below
- v_scales: float32 [4, 8, 704], P('freq', 'tile'), as said below
- tile_ranks: int32 [4, 8, 8], P('freq'), may hold values from 40 to 88, as said below
- mute_start: int32 [4096], P('tile'), may hold values from 0 to 64
Outputs:
- gradient_time: bfloat16 [4096, 128, 128], P('tile', 'freq')
Inputs may be any that keep to these rules, and one draw needn't show every extreme that they name: `tile_ranks`: for every frequency the ranks are symmetric; one tile row (and column), drawn per frequency, has every tile of rank 88, so its total is exactly 704; no row or column totals more. `u_codes`: whole numbers. `v_codes`: whole numbers. `u_scales`: Positive. `v_scales`: Positive.
All inputs are finite; a program needn't handle non-finite values.
Results may differ from a plain program's by a relative error of at most 0.0075.
Values may be sent and summed in bfloat16 or wider, within the bound.
A program may use at most 128 MiB of HBM per device.

v0:
```python
import math

import jax
import jax.numpy as jnp
from jax import lax
from jax.sharding import PartitionSpec as P

RSLOT = 88
NTIME = 128


def unpack_pool(code_vals, scale_row):
    return (code_vals.astype(jnp.float32) * scale_row).astype(jnp.bfloat16)


def apply_factor(factor, pooled):
    half_width = pooled.shape[1] // 2
    real_part = jnp.dot(factor[0], pooled, preferred_element_type=jnp.float32)
    imag_part = jnp.dot(factor[1], pooled, preferred_element_type=jnp.float32)
    out_re = real_part[:, :half_width] - imag_part[:, half_width:]
    out_im = real_part[:, half_width:] + imag_part[:, :half_width]
    return jnp.concatenate([out_re, out_im], 1)


def apply_adjoint(factor, dense_rows):
    half_width = dense_rows.shape[1] // 2
    dims = (((0,), (0,)), ((), ()))
    real_part = lax.dot_general(factor[0], dense_rows, dims, preferred_element_type=jnp.float32)
    imag_part = lax.dot_general(factor[1], dense_rows, dims, preferred_element_type=jnp.float32)
    out_re = real_part[:, :half_width] + imag_part[:, half_width:]
    out_im = real_part[:, half_width:] - imag_part[:, :half_width]
    return jnp.concatenate([out_re, out_im], 1)


def pool_owner(ends, begins, capacity, tile_count):
    column = jnp.arange(capacity, dtype=jnp.int32)
    owner_raw = jnp.sum((column[:, None] >= ends[None, :]).astype(jnp.int32), 1)
    is_live = owner_raw < tile_count
    owner_tile = jnp.minimum(owner_raw, tile_count - 1)
    offset = column - begins[owner_tile]
    return (owner_tile, offset, is_live)


def fill_slots(pooled, begins, rank_vec):
    slot_pos = jnp.arange(RSLOT, dtype=jnp.int32)
    is_live = slot_pos[None, :] < rank_vec[:, None]
    source = jnp.where(is_live, begins[:, None] + slot_pos[None, :], 0)
    picked = pooled[source.reshape(-1)].reshape(rank_vec.shape[0], RSLOT, pooled.shape[1])
    return jnp.where(is_live[:, :, None], picked, 0)


def pool_from_slots(arrived, ends, begins, capacity):
    tile_count = arrived.shape[0]
    flat_slots = arrived.reshape(tile_count * RSLOT, arrived.shape[2])
    owner_tile, offset, is_live = pool_owner(ends, begins, capacity, tile_count)
    source = jnp.where(is_live, owner_tile * RSLOT + offset, 0)
    return jnp.where(is_live[:, None], flat_slots[source], 0)


def shards(model_field, data_field, u_codes, u_scales, v_codes, v_scales, tile_ranks, mute_start):
    my_tile = lax.axis_index("tile")
    rank_table = tile_ranks[0]
    row_ranks = rank_table[my_tile]
    col_ranks = rank_table[:, my_tile]
    row_end = jnp.cumsum(row_ranks)
    row_begin = row_end - row_ranks
    col_end = jnp.cumsum(col_ranks)
    col_begin = col_end - col_ranks
    v_factor = unpack_pool(v_codes[0], v_scales[0, 0])
    u_factor = unpack_pool(u_codes[0], u_scales[0, 0])
    capacity = v_factor.shape[2]
    rows_here = model_field.shape[1]
    sources = model_field.shape[2] // 2
    w_pool = apply_adjoint(v_factor, model_field[0]).astype(jnp.bfloat16)
    w_slots = fill_slots(w_pool, col_begin, col_ranks)
    w_arrived = lax.all_to_all(w_slots, "tile", split_axis=0, concat_axis=0, tiled=True)
    w_rows = pool_from_slots(w_arrived, row_end, row_begin, capacity)
    predicted = apply_factor(u_factor, w_rows)
    residual = (predicted - data_field[0].astype(jnp.float32)).astype(jnp.bfloat16)
    p_pool = apply_adjoint(u_factor, residual).astype(jnp.bfloat16)
    p_slots = fill_slots(p_pool, row_begin, row_ranks)
    p_arrived = lax.all_to_all(p_slots, "tile", split_axis=0, concat_axis=0, tiled=True)
    p_cols = pool_from_slots(p_arrived, col_end, col_begin, capacity)
    gradient = apply_factor(v_factor, p_cols).astype(jnp.bfloat16)
    freq_count = lax.axis_size("freq")
    share = sources // freq_count
    sectioned = gradient.reshape(1, rows_here, 2, freq_count, share)
    arrived = lax.all_to_all(sectioned, "freq", split_axis=3, concat_axis=0, tiled=True)
    spectra = arrived.reshape(freq_count, rows_here, 2, share).astype(jnp.float32)
    freq_bin = jnp.arange(freq_count, dtype=jnp.int32).astype(jnp.float32) + 1.0
    time_grid = jnp.arange(NTIME, dtype=jnp.int32).astype(jnp.float32)
    phase_arg = 2.0 * math.pi * freq_bin[:, None] * time_grid[None, :] / NTIME
    time_basis = jnp.stack([jnp.cos(phase_arg), -jnp.sin(phase_arg)], 1)
    signal = 0.5 * jnp.einsum("fncs,fct->nst", spectra, time_basis, precision=lax.Precision.HIGHEST)
    unmuted = jnp.arange(NTIME, dtype=jnp.int32)[None, None, :] >= mute_start[:, None, None]
    return jnp.where(unmuted, signal, 0.0).astype(jnp.bfloat16)


def solution(mesh):
    in_specs = (
        P("freq", "tile", None),
        P("freq", "tile", None),
        P("freq", None, "tile", None),
        P("freq", "tile", None),
        P("freq", None, "tile", None),
        P("freq", "tile", None),
        P("freq", None, None),
        P("tile"),
    )
    out_specs = P("tile", "freq", None)
    return jax.shard_map(shards, mesh=mesh, in_specs=in_specs, out_specs=out_specs, check_vma=False)
```

profile of v0, /device:TPU:0, one launch (start us, length us, event | category | flops | bytes accessed | tf_op | source)
XLA Modules:
  0.0 80.9 jit_solution(18117013231912383431)
XLA Ops:
  0.0 0.0 copy-start
  0.0 0.7 reduce
  0.7 1.7 %fusion.3 = bf16[2,512,704]{1,2,0:T(8,128)(2,1)S(1)} fusion(bf16[1,2,512,704]{2,3,1,0:T(8,128)(2,1)} %param.12, f32[704]{0:T(1024)S(1)} %reduce), kind=kLoop, calls=%fused_computation.10 | loop fusion | flops 2162688 | bytes 2886400 | tf_op jit(solution)/shard_map/convert_element_type | solution.py:13
  2.4 0.0 copy-done
  2.4 0.0 copy-start.4
  2.4 0.3 fusion.9
  2.8 0.3 fusion.5
  3.2 0.0 copy-done.4
  3.2 0.2 dynamic-slice_reduce_fusion
  3.3 0.1 iota_compare_fusion.3
  3.4 0.2 reduce-window.14
  3.6 0.1 add_select_fusion.1
  3.7 0.1 select_n.134
  3.8 0.1 fusion.16
  3.9 2.8 %gather_fusion = bf16[704,256]{1,0:T(8,128)(2,1)S(1)} fusion(bf16[704,256]{1,0:T(8,128)(2,1)S(1)} %pad_maximum_fusion, s32[1024]{0:T(1024)S(1)} %pad_clamp_fusion.3), kind=kCustom, calls=%fused_computation | custom fusion | bytes 723712 | tf_op jit(solution)/shard_map/gather | solution.py:48
  6.8 0.0 copy-start.5
  6.8 0.0 copy-start.3
  6.8 0.9 %broadcast_select_fusion.2 = bf16[8,88,256]{2,1,0:T(8,128)(2,1)} fusion(bf16[8,88,256]{2,1,0:T(8,128)(2,1)S(1)} %bitcast.85, pred[8,88]{1,0:T(8,128)(4,1)S(1)} %iota_compare_fusion.3), kind=kLoop, calls=%fused_computation.37 | loop fusion | flops 180224 | bytes 721600 | tf_op jit(solution)/shard_map/jit(_where)/select_n | solution.py:49
  7.7 7.3 %all-to-all-start = ((bf16[8,88,256]{2,1,0:T(8,128)(2,1)}), bf16[8,88,256]{2,1,0:T(8,128)(2,1)S(1)}, u32[]{:S(2)}, u32[]{:S(2)}) async-start(bf16[8,88,256]{2,1,0:T(8,128)(2,1)} %broadcast_select_fusion.2), calls=%async_computation | async-start | bytes 720896 | tf_op jit(solution)/shard_map/all_to_all | solution.py:76
  15.0 0.2 reduce-window.15
  15.2 0.1 iota_compare_fusion.4
  15.2 0.1 add_select_fusion
  15.3 0.7 fusion.46
  16.0 0.7 fusion.45
  16.7 0.1 convert_reduce_fusion
  16.8 0.1 select_n.142
  17.0 0.1 convert_reduce_fusion.1
  17.1 0.0 copy-done.5
  17.1 0.0 copy-done.3
  17.1 0.8 %copy.16 = bf16[1,512,256]{1,2,0:T(8,128)(2,1)} copy(bf16[1,512,256]{2,1,0:T(8,128)(2,1)S(1)} %copy-done.3) | data formatting | bytes 524288 | tf_op args[1]
  18.0 4.4 %fusion.28 = s32[704]{0:T(1024)S(1)} fusion(s32[]{:T(128)} %bitcast.13, s32[]{:T(128)} %bitcast.14, s32[]{:T(128)} %bitcast.15, s32[]{:T(128)} %bitcast.16, s32[]{:T(128)} %bitcast.17, s32[]{:T(128)} %bitcast.19, s32[]{:T(128)} %bitcast.18, s32[704]{0:T(1024)S(1)} %broadcast_minimum_fusion.1), kind=kLoop, calls=%fused_computation.92 | loop fusion | flops 10560 | bytes 5660 | tf_op jit(solution)/shard_map/gather | solution.py:40
  22.3 0.6 broadcast_select_fusion.9
  23.0 4.5 %fusion.29 = s32[704]{0:T(1024)S(1)} fusion(s32[]{:T(128)} %bitcast.27, s32[]{:T(128)} %bitcast.28, s32[]{:T(128)} %bitcast.29, s32[]{:T(128)} %bitcast.30, s32[]{:T(128)} %bitcast.31, s32[]{:T(128)} %bitcast.33, s32[]{:T(128)} %bitcast.32, s32[704]{0:T(1024)S(1)} %broadcast_minimum_fusion), kind=kLoop, calls=%fused_computation.93 | loop fusion | flops 10560 | bytes 5660 | tf_op jit(solution)/shard_map/gather | solution.py:40
  27.5 0.6 broadcast_select_fusion.8
  28.2 1.7 %fusion.2 = bf16[2,512,704]{1,2,0:T(8,128)(2,1)S(1)} fusion(bf16[1,2,512,704]{2,3,1,0:T(8,128)(2,1)} %param.10, f32[704]{0:T(1024)S(1)} %reduce.2), kind=kLoop, calls=%fused_computation.8 | loop fusion | flops 2162688 | bytes 2886400 | tf_op jit(solution)/shard_map/convert_element_type | solution.py:13
  29.8 0.0 all-to-all-done
  29.8 3.3 %gather_fusion.1 = bf16[704,256]{1,0:T(8,128)(2,1)} fusion(bf16[704,256]{1,0:T(8,128)(2,1)S(1)} %bitcast.83, s32[1024]{0:T(1024)S(1)} %pad_clamp_fusion.2), kind=kCustom, calls=%fused_computation.1 | custom fusion | bytes 723712 | tf_op jit(solution)/shard_map/gather | solution.py:57
  33.1 0.0 copy-start.2
  33.1 1.6 %fusion.11 = f32[512,256]{0,1:T(8,128)S(1)} fusion(bf16[2,512,704]{1,2,0:T(8,128)(2,1)S(1)} %fusion.2, bf16[704,256]{1,0:T(8,128)(2,1)} %gather_fusion.1, pred[704]{0:T(1024)(128)(4,1)S(1)} %broadcast_compare_fusion), kind=kOutput, calls=%fused_computation.22 | convolution fusion | flops 184729600 | bytes 1606656 | tf_op jit(solution)/shard_map/dot_general | solution.py:19
  34.8 0.0 copy-done.2
  34.8 0.0 copy-start.1
  34.8 0.6 fusion.7
  35.4 0.1 fusion.21
  35.5 0.3 copy-done.1
  35.7 0.4 fusion.10
  36.1 0.4 fusion.6
  36.5 0.1 fusion.14
  36.6 2.8 %gather_fusion.2 = bf16[704,256]{1,0:T(8,128)(2,1)S(1)} fusion(bf16[704,256]{1,0:T(8,128)(2,1)S(1)} %pad_maximum_fusion.1, s32[1024]{0:T(1024)S(1)} %pad_clamp_fusion.1), kind=kCustom, calls=%fused_computation.2 | custom fusion | bytes 723712 | tf_op jit(solution)/shard_map/gather | solution.py:48
  39.5 0.0 copy-start.6
  39.5 0.9 %broadcast_select_fusion.3 = bf16[8,88,256]{2,1,0:T(8,128)(2,1)} fusion(bf16[8,88,256]{2,1,0:T(8,128)(2,1)S(1)} %bitcast.86, pred[8,88]{1,0:T(8,128)(4,1)S(1)} %iota_compare_fusion.4), kind=kLoop, calls=%fused_computation.38 | loop fusion | flops 180224 | bytes 721600 | tf_op jit(solution)/shard_map/jit(_where)/select_n | solution.py:49
  40.4 6.0 %all-to-all-start.1 = ((bf16[8,88,256]{2,1,0:T(8,128)(2,1)}), bf16[8,88,256]{2,1,0:T(8,128)(2,1)S(1)}, u32[]{:S(2)}, u32[]{:S(2)}) async-start(bf16[8,88,256]{2,1,0:T(8,128)(2,1)} %broadcast_select_fusion.3), calls=%async_computation.1 | async-start | bytes 720896 | tf_op jit(solution)/shard_map/all_to_all | solution.py:82
  46.4 0.0 copy-done.6
  46.4 0.1 iota_compare_fusion
  46.6 10.2 %all-to-all-done.1 = bf16[8,88,256]{2,1,0:T(8,128)(2,1)S(1)} async-done(((bf16[8,88,256]{2,1,0:T(8,128)(2,1)}), bf16[8,88,256]{2,1,0:T(8,128)(2,1)S(1)}, u32[]{:S(2)}, u32[]{:S(2)}) %all-to-all-start.1) | async-done | bytes 360480 | tf_op jit(solution)/shard_map/all_to_all | solution.py:82
  56.8 2.8 %gather_fusion.3 = bf16[704,256]{1,0:T(8,128)(2,1)S(1)} fusion(bf16[704,256]{1,0:T(8,128)(2,1)S(1)} %bitcast.84, s32[1024]{0:T(1024)S(1)} %pad_clamp_fusion), kind=kCustom, calls=%fused_computation.3 | custom fusion | bytes 723712 | tf_op jit(solution)/shard_map/gather | solution.py:57
  59.6 0.6 fusion.8
  60.2 0.6 fusion.4
  60.8 0.1 fusion.19
  60.9 1.0 %copy.17 = bf16[1,512,2,4,32]{1,2,4,0,3:T(2,128)(2,1)} copy(bf16[1,512,2,4,32]{1,4,3,2,0:T(8,128)(2,1)S(1)} %bitcast.87) | data formatting | bytes 524288 | tf_op jit(solution)/shard_map/convert_element_type | solution.py:84
  61.9 3.6 %all-to-all-start.2 = ((bf16[1,512,2,4,32]{1,2,4,0,3:T(2,128)(2,1)}), bf16[1,512,2,4,32]{1,2,4,0,3:T(2,128)(2,1)S(1)}, u32[]{:S(2)}, u32[]{:S(2)}) async-start(bf16[1,512,2,4,32]{1,2,4,0,3:T(2,128)(2,1)} %copy.17), calls=%async_computation.2 | async-start | bytes 524288 | tf_op jit(solution)/shard_map/all_to_all | solution.py:88
  65.5 0.1 fusion.34
  65.6 5.7 %all-to-all-done.2 = bf16[1,512,2,4,32]{1,2,4,0,3:T(2,128)(2,1)S(1)} async-done(((bf16[1,512,2,4,32]{1,2,4,0,3:T(2,128)(2,1)}), bf16[1,512,2,4,32]{1,2,4,0,3:T(2,128)(2,1)S(1)}, u32[]{:S(2)}, u32[]{:S(2)}) %all-to-all-start.2) | async-done | bytes 262176 | tf_op jit(solution)/shard_map/all_to_all | solution.py:88
  71.3 4.9 %fusion.1 = bf16[512,32,128]{2,0,1:T(8,128)(2,1)S(1)} fusion(pred[512,128]{1,0:T(8,128)(4,1)S(1)} %iota_compare_fusion, bf16[1,512,2,4,32]{1,2,4,0,3:T(2,128)(2,1)S(1)} %all-to-all-done.2, f32[4,1,128]{2,0,1:T(4,128)S(1)} %get-tuple-element.16, f32[4,1,128]{2,0,1:T(4,128)S(1)} %get-tuple-element.15), kind=kOutput, calls=%fused_computation.6 | convolution fusion | flops 207619072 | bytes 4526080 | tf_op jit(solution)/shard_map/fncs,fct->nst/dot_general | solution.py:94
  76.2 4.7 %copy.19 = bf16[512,32,128]{2,1,0:T(8,128)(2,1)} copy(bf16[512,32,128]{2,0,1:T(8,128)(2,1)S(1)} %fusion.1) | data formatting | bytes 8388608 | tf_op jit(solution)/shard_map/convert_element_type | solution.py:96
  (23 shorter events, 0.3 us)
Async XLA Ops:
  0.0 2.4 %copy-start = (bf16[1,512,256]{2,1,0:T(8,128)(2,1)S(1)}, bf16[1,512,256]{2,1,0:T(8,128)(2,1)}, u32[]{:S(2)}) copy-start(bf16[1,512,256]{2,1,0:T(8,128)(2,1)} %param.8) | copy-start | bytes 786436
  2.4 0.7 copy-start.4
  6.8 10.3 %copy-start.5 = (f32[1,1,704]{2,1,0:T(1,128)S(1)}, f32[1,1,704]{2,1,0:T(1,128)}, u32[]{:S(2)}) copy-start(f32[1,1,704]{2,1,0:T(1,128)} %param.11) | copy-start | bytes 8452
  6.8 10.3 %copy-start.3 = (bf16[1,512,256]{2,1,0:T(8,128)(2,1)S(1)}, bf16[1,512,256]{2,1,0:T(8,128)(2,1)}, u32[]{:S(2)}) copy-start(bf16[1,512,256]{2,1,0:T(8,128)(2,1)} %param.9) | copy-start | bytes 786436
  7.7 22.1 %all-to-all-start = ((bf16[8,88,256]{2,1,0:T(8,128)(2,1)}), bf16[8,88,256]{2,1,0:T(8,128)(2,1)S(1)}, u32[]{:S(2)}, u32[]{:S(2)}) async-start(bf16[8,88,256]{2,1,0:T(8,128)(2,1)} %broadcast_select_fusion.2), calls=%async_computation | async-start | bytes 720896 | tf_op jit(solution)/shard_map/all_to_all | solution.py:76
  33.1 1.6 %copy-start.2 = (bf16[704,256]{1,0:T(8,128)(2,1)S(1)}, bf16[704,256]{1,0:T(8,128)(2,1)}, u32[]{:S(2)}) copy-start(bf16[704,256]{1,0:T(8,128)(2,1)} %gather_fusion.1) | copy-start | bytes 1081348
  34.8 1.0 %copy-start.1 = (bf16[1,512,256]{1,2,0:T(8,128)(2,1)S(1)}, bf16[1,512,256]{1,2,0:T(8,128)(2,1)}, u32[]{:S(2)}) copy-start(bf16[1,512,256]{1,2,0:T(8,128)(2,1)} %copy.16) | copy-start | bytes 786436
  39.5 7.0 %copy-start.6 = (s32[512]{0:T(512)S(1)}, s32[512]{0:T(512)}, u32[]{:S(2)}) copy-start(s32[512]{0:T(512)} %param.15) | copy-start | bytes 6148
  40.4 16.4 %all-to-all-start.1 = ((bf16[8,88,256]{2,1,0:T(8,128)(2,1)}), bf16[8,88,256]{2,1,0:T(8,128)(2,1)S(1)}, u32[]{:S(2)}, u32[]{:S(2)}) async-start(bf16[8,88,256]{2,1,0:T(8,128)(2,1)} %broadcast_select_fusion.3), calls=%async_computation.1 | async-start | bytes 720896 | tf_op jit(solution)/shard_map/all_to_all | solution.py:82
  61.9 9.4 %all-to-all-start.2 = ((bf16[1,512,2,4,32]{1,2,4,0,3:T(2,128)(2,1)}), bf16[1,512,2,4,32]{1,2,4,0,3:T(2,128)(2,1)S(1)}, u32[]{:S(2)}, u32[]{:S(2)}) async-start(bf16[1,512,2,4,32]{1,2,4,0,3:T(2,128)(2,1)} %copy.17), calls=%async_computation.2 | async-start | bytes 524288 | tf_op jit(solution)/shard_map/all_to_all | solution.py:88
where the time goes:
time: 81.6 us; the launch traced here: 80.9 us
  local copies, waits for them, and re-layouts  20.3 us (25%)
  other arithmetic  17.7 us (22%)
  starting transfers between devices  16.9 us (21%)
  waiting for transfers between devices  15.9 us (19%)
  matrix products  9.73 us (12%)
    all_to_all x1, waiting for transfers between devices, shards(): lax.all_to_all(p_slots, 'tile', split_axis=0, concat_axis=0, tiled=True)  10.2 us
    gather x6, other arithmetic, pool_owner(): offset = column - begins[owner_tile]  10.2 us
    all_to_all x1, starting transfers between devices, shards(): lax.all_to_all(w_slots, 'tile', split_axis=0, concat_axis=0, tiled=True)  7.28 us
    gather x2, local copies, waits for them, and re-layouts, pool_from_slots(): return jnp.where(is_live[:, None], flat_slots[source], 0)  6.07 us
    all_to_all x1, starting transfers between devices, shards(): lax.all_to_all(p_slots, 'tile', split_axis=0, concat_axis=0, tiled=True)  6 us
    all_to_all x1, waiting for transfers between devices, shards(): lax.all_to_all(sectioned, 'freq', split_axis=3, concat_axis=0, tiled=True)  5.71 us
    gather x2, local copies, waits for them, and re-layouts, fill_slots(): pooled[source.reshape(-1)]  5.63 us
    dot_general x1, matrix products, shards(): jnp.einsum('fncs,fct->nst', spectra, time_basis, precision=lax.Precision....  4.89 us
  transfers between devices with their start and end apart: 3, of which 2 were waited for; matrix products, arithmetic and copies ran while one was open for 19% of the time, Pallas kernels for 0%

commit v1 on v0

v1 whole, which is shorter than its diff:
```python
import functools
import math

import jax
import jax.numpy as jnp
import numpy as np
from jax import lax
from jax.experimental import pallas as pl
from jax.experimental.pallas import tpu as pltpu
from jax.sharding import PartitionSpec as P

NTIME = 128
HALVES = 2
BF = jnp.bfloat16
F32 = jnp.float32
MESH = pl.DeviceIdType.MESH
NT_DIMS = (((1,), (1,)), ((), ()))


def dot_nn(a, b):
    return jnp.dot(a, b, preferred_element_type=F32)


def dot_nt(a, b):
    return lax.dot_general(a, b, NT_DIMS, preferred_element_type=F32)


def exchange_kernel(
    tiles,
    freqs,
    ranks,
    model_hbm,
    data_hbm,
    ucodes_hbm,
    uscale,
    vcodes_hbm,
    vscale,
    out,
    model,
    data,
    ufac,
    vfac,
    sel,
    wt,
    uslot,
    uslot_t,
    vslot,
    dperm,
    pool,
    resid,
    sbuf,
    rbuf,
    fsend,
    frecv,
    load_sem,
    send_sem,
    recv_sem,
    fsend_sem,
    frecv_sem,
):
    tile = lax.axis_index("tile")
    freq = lax.axis_index("freq")
    rows, cols = model.shape
    lanes = cols // HALVES
    cap = ufac.shape[2]
    slot = cap // tiles
    pad = pool.shape[0] // tiles
    group = sel.shape[0] // pad
    groups = tiles // group
    part = lanes // freqs // 2
    brows = rows // freqs

    loads = [
        pltpu.make_async_copy(src, dst, load_sem.at[k])
        for k, (src, dst) in enumerate(
            [
                (model_hbm, model),
                (vcodes_hbm, vfac),
                (ucodes_hbm, ufac),
                (data_hbm, data),
            ]
        )
    ]
    for load in loads:
        load.start()

    barrier = pltpu.get_barrier_semaphore()
    for d in range(1, tiles):
        pl.semaphore_signal(
            barrier, inc=1, device_id=(freq, lax.rem(tile + d, tiles)), device_id_type=MESH
        )
    for d in range(1, freqs):
        pl.semaphore_signal(
            barrier, inc=1, device_id=(lax.rem(freq + d, freqs), tile), device_id_type=MESH
        )

    own = [ranks[i, tile] for i in range(tiles)]
    begins = []
    run = jnp.int32(0)
    for i in range(tiles):
        begins.append(run)
        run = run + own[i]

    def build_sel(g):
        k = lax.broadcasted_iota(jnp.int32, (pad, cap), 0)
        diff = lax.broadcasted_iota(jnp.int32, (pad, cap), 1) - k
        for b in range(group):
            i = g * group + b
            hit = (diff == begins[i]) & (k < own[i])
            sel[b * pad : (b + 1) * pad, :] = jnp.where(hit, 1.0, 0.0).astype(BF)

    def block_perm():
        p = lax.broadcasted_iota(jnp.int32, (cols, cols), 0)
        c = lax.broadcasted_iota(jnp.int32, (cols, cols), 1)
        half = p // lanes
        comp = (p % lanes) // (lanes // 2)
        share = (p % (lanes // 2)) // part
        nat = comp * (cols // 2) + share * (2 * part) + half * part + p % part
        return jnp.where(c == nat, 1.0, 0.0).astype(BF)

    build_sel(0)
    perm = block_perm()
    pool[...] = jnp.zeros_like(pool)
    loads[0].wait()
    mt = dot_nt(perm, model[...]).astype(BF)

    step = rows // 4

    def unpack(fac, scale):
        s = scale[...]

        def body(r, carry):
            for c in range(2):
                at = pl.ds(pl.multiple_of(r * step, step), step)
                fac[c, at, :] = (fac[c, at, :].astype(F32) * s).astype(BF)
            return carry

        lax.fori_loop(0, rows // step, body, 0)

    loads[1].wait()
    unpack(vfac, vscale)
    a = dot_nn(mt, vfac[0])
    b = dot_nn(mt, vfac[1])
    hl = lanes // 2
    for h in range(HALVES):
        o = h * lanes
        wt[o : o + hl, :] = (a[o : o + hl] + b[o + hl : o + lanes]).astype(BF)
        wt[o + hl : o + lanes, :] = (a[o + hl : o + lanes] - b[o : o + hl]).astype(BF)
    for g in range(groups):
        if groups > 1:
            build_sel(g)
        for h in range(HALVES):
            w = dot_nt(sel[...], wt[h * lanes : (h + 1) * lanes, :]).astype(BF)
            for k in range(group):
                sbuf[0, h, g * group + k] = w[k * pad : k * pad + slot]

    pl.semaphore_wait(barrier, tiles - 1 + freqs - 1)

    def block_copy(phase, h, d):
        dst = lax.rem(tile + d, tiles)
        return pltpu.make_async_remote_copy(
            src_ref=sbuf.at[phase, h, dst],
            dst_ref=rbuf.at[phase, h, tile],
            send_sem=send_sem.at[phase, h, dst],
            recv_sem=recv_sem.at[phase, h, tile],
            device_id=(freq, dst),
            device_id_type=MESH,
        )

    def block_arrival(phase, h, d):
        src = lax.rem(tile + d, tiles)
        return pltpu.make_async_remote_copy(
            src_ref=sbuf.at[phase, h, src],
            dst_ref=rbuf.at[phase, h, src],
            send_sem=send_sem.at[phase, h, src],
            recv_sem=recv_sem.at[phase, h, src],
            device_id=(freq, src),
            device_id_type=MESH,
        )

    def send_blocks(phase, h):
        for d in range(1, tiles):
            block_copy(phase, h, d).start()
        rbuf[phase, h, tile] = sbuf[phase, h, tile]

    def take_blocks(phase, h):
        for d in range(1, tiles):
            block_arrival(phase, h, d).wait_recv()
        for i in range(tiles):
            pool[i * pad : i * pad + slot, :] = rbuf[phase, h, i]

    send_blocks(0, 0)
    send_blocks(0, 1)

    lane = lax.broadcasted_iota(jnp.int32, (1, lanes), 1)
    sign = jnp.where(lane < hl, 1.0, -1.0).astype(F32)

    half_rows = rows // 2
    slots = pool.shape[0]
    srows = group * pad

    def to_slots(fac, slots_ref, slots_t_ref):
        for g in range(groups):
            if groups > 1:
                build_sel(g)

            for r in range(2):
                at = slice(r * half_rows, (r + 1) * half_rows)
                for c in range(2):
                    x = fac[c, at, :]
                    slots_ref[c, at, g * srows : (g + 1) * srows] = dot_nt(x, sel[...]).astype(BF)
                    if slots_t_ref is not None:
                        slots_t_ref[c, g * srows : (g + 1) * srows, at] = dot_nt(sel[...], x).astype(BF)

    loads[2].wait()
    unpack(ufac, uscale)
    to_slots(ufac, uslot, uslot_t)
    loads[3].wait()
    dperm[...] = dot_nt(data[...], perm)

    for h in range(HALVES):
        take_blocks(0, h)
        w = pool[...]
        re = dot_nn(uslot[0], w)
        im = dot_nn(uslot[1], w)
        y = re - sign * pltpu.roll(im, hl, 1)
        resid[...] = (y - dperm[:, h * lanes : (h + 1) * lanes]).astype(BF)
        x = resid[...]
        re = dot_nn(uslot_t[0], x)
        im = dot_nn(uslot_t[1], x)
        p = (re + sign * pltpu.roll(im, hl, 1)).astype(BF)
        for i in range(tiles):
            sbuf[1, h, i] = p[i * pad : i * pad + slot]
        send_blocks(1, h)
        if h == 0:
            to_slots(vfac, vslot, None)

    def swap_groups(pieces):
        out_pieces = []
        where_g = (lane % hl) // part
        for q in range(freqs):
            acc = pieces[0] if q == 0 else pltpu.roll(pieces[0], (lanes - q * part) % lanes, 1)
            for g in range(1, freqs):
                shift = (g - q) * part % lanes
                moved = pieces[g] if shift == 0 else pltpu.roll(pieces[g], shift, 1)
                acc = jnp.where(where_g == g, moved, acc)
            out_pieces.append(acc)
        return out_pieces

    def share_copy(h, d, arrival):
        other = lax.rem(freq + d, freqs)
        slot_at = other if arrival else freq
        return pltpu.make_async_remote_copy(
            src_ref=fsend.at[h, other],
            dst_ref=frecv.at[h, slot_at],
            send_sem=fsend_sem.at[h, other],
            recv_sem=frecv_sem.at[h, slot_at],
            device_id=(other, tile),
            device_id_type=MESH,
        )

    for h in range(HALVES):
        take_blocks(1, h)
        w = pool[...]
        re = dot_nn(vslot[0], w)
        im = dot_nn(vslot[1], w)
        grad = re - sign * pltpu.roll(im, hl, 1)
        packed = swap_groups([grad[g * brows : (g + 1) * brows] for g in range(freqs)])
        for q in range(freqs):
            fsend[h, q] = packed[q].astype(BF)
        for d in range(1, freqs):
            share_copy(h, d, False).start()
        frecv[h, freq] = fsend[h, freq]

    for h in range(HALVES):
        for d in range(1, freqs):
            share_copy(h, d, True).wait_recv()
        parts = swap_groups([frecv[h, f].astype(F32) for f in range(freqs)])
        for g in range(freqs):
            out[g * brows : (g + 1) * brows, h * lanes : (h + 1) * lanes] = parts[g]

    for h in range(HALVES):
        for phase in range(2):
            for d in range(1, tiles):
                block_copy(phase, h, d).wait_send()
        for d in range(1, freqs):
            share_copy(h, d, False).wait_send()


def time_kernel(share, freqs, mute, spec, basis, out):
    block = spec.shape[0]
    depth = spec.shape[1]
    start = pl.program_id(0) * block
    half = depth // HALVES
    part = share // HALVES
    s = lax.broadcasted_iota(jnp.int32, (share, depth), 0)
    k = lax.broadcasted_iota(jnp.int32, (share, depth), 1)
    keep = (k // half == s // part) & (k % part == s % part)
    mask = jnp.where(keep, 1.0, 0.0).astype(BF)
    table = basis[...]
    t = lax.broadcasted_iota(jnp.int32, (share, NTIME), 1)
    batch = 8
    for n0 in range(0, block, batch):
        rows = []
        for n in range(n0, n0 + batch):
            row = jnp.broadcast_to(spec[n : n + 1, :], (share, depth)).astype(BF)
            rows.append(row * mask)
        both = dot_nn(jnp.concatenate(rows, 0), table)
        signal = both[:, :NTIME] + both[:, NTIME:]
        for n in range(n0, n0 + batch):
            o = (n - n0) * share
            live = t >= mute[start + n]
            out[n] = jnp.where(live, signal[o : o + share], 0.0).astype(BF)


def time_table(freqs, share):
    part = share // HALVES
    k = np.arange(2 * share * freqs)
    f = (k % (part * freqs)) // part
    c = (k % (2 * part * freqs)) // (part * freqs)
    angle = 2.0 * math.pi * (f[:, None] + 1) * np.arange(NTIME)[None, :] / NTIME
    table = 0.5 * np.where(c[:, None] == 0, np.cos(angle), -np.sin(angle))
    high = table.astype(jnp.bfloat16)
    low = (table - high.astype(np.float64)).astype(jnp.bfloat16)
    return np.concatenate([high, low], 1)


def shards(tiles, freqs, model_field, data_field, u_codes, u_scales, v_codes, v_scales, tile_ranks, mute_start):
    rows, cols = model_field.shape[1:]
    cap = u_codes.shape[3]
    slot = cap // tiles
    pad = -(-slot // 32) * 32
    slots = tiles * pad
    group = min(tiles, 8)
    lanes = cols // HALVES
    share = cols // 2 // freqs
    brows = rows // freqs
    any_spec = pl.BlockSpec(memory_space=pl.ANY)
    vmem = pl.BlockSpec(memory_space=pltpu.VMEM)
    smem = pl.BlockSpec(memory_space=pltpu.SMEM)
    spectra = pl.pallas_call(
        functools.partial(exchange_kernel, tiles, freqs),
        out_shape=jax.ShapeDtypeStruct((rows, cols), F32),
        in_specs=[smem, any_spec, any_spec, any_spec, vmem, any_spec, vmem],
        out_specs=vmem,
        scratch_shapes=[
            pltpu.VMEM((rows, cols), BF),
            pltpu.VMEM((rows, cols), BF),
            pltpu.VMEM((2, rows, cap), BF),
            pltpu.VMEM((2, rows, cap), BF),
            pltpu.VMEM((group * pad, cap), BF),
            pltpu.VMEM((cols, cap), BF),
            pltpu.VMEM((2, rows, slots), BF),
            pltpu.VMEM((2, slots, rows), BF),
            pltpu.VMEM((2, rows, slots), BF),
            pltpu.VMEM((rows, cols), F32),
            pltpu.VMEM((slots, lanes), BF),
            pltpu.VMEM((rows, lanes), BF),
            pltpu.VMEM((2, HALVES, tiles, slot, lanes), BF),
            pltpu.VMEM((2, HALVES, tiles, slot, lanes), BF),
            pltpu.VMEM((HALVES, freqs, brows, lanes), BF),
            pltpu.VMEM((HALVES, freqs, brows, lanes), BF),
            pltpu.SemaphoreType.DMA((4,)),
            pltpu.SemaphoreType.DMA((2, HALVES, tiles)),
            pltpu.SemaphoreType.DMA((2, HALVES, tiles)),
            pltpu.SemaphoreType.DMA((HALVES, freqs)),
            pltpu.SemaphoreType.DMA((HALVES, freqs)),
        ],
        compiler_params=pltpu.CompilerParams(
            collective_id=0, has_side_effects=True, vmem_limit_bytes=60 * 2**20
        ),
        cost_estimate=pl.CostEstimate(
            flops=16 * rows * cap * cols, bytes_accessed=8 * rows * cap, transcendentals=0
        ),
        name="exchange",
    )(tile_ranks[0], model_field[0], data_field[0], u_codes[0], u_scales[0], v_codes[0], v_scales[0])
    table = jnp.asarray(time_table(freqs, share))
    block = 64
    return pl.pallas_call(
        functools.partial(time_kernel, share, freqs),
        out_shape=jax.ShapeDtypeStruct((rows, share, NTIME), BF),
        grid=(rows // block,),
        in_specs=[
            smem,
            pl.BlockSpec((block, cols), lambda i: (i, 0)),
            pl.BlockSpec((cols, 2 * NTIME), lambda i: (0, 0)),
        ],
        out_specs=pl.BlockSpec((block, share, NTIME), lambda i: (i, 0, 0)),
        compiler_params=pltpu.CompilerParams(vmem_limit_bytes=32 * 2**20),
        name="to_time",
    )(mute_start, spectra, table)


def solution(mesh):
    in_specs = (
        P("freq", "tile", None),
        P("freq", "tile", None),
        P("freq", None, "tile", None),
        P("freq", "tile", None),
        P("freq", None, "tile", None),
        P("freq", "tile", None),
        P("freq", None, None),
        P("tile"),
    )
    step = functools.partial(shards, mesh.shape["tile"], mesh.shape["freq"])
    return jax.shard_map(step, mesh=mesh, in_specs=in_specs, out_specs=P("tile", "freq", None), check_vma=False)
```

time: 81.6 us -> 41.7 us (0.51)
  Pallas kernels: 0 us -> 36.2 us
  other arithmetic: 17.7 us -> 0 us
  starting transfers between devices: 16.9 us -> 0 us
  waiting for transfers between devices: 15.9 us -> 0 us
  local copies, waits for them, and re-layouts: 20.3 us -> 5.27 us
  matrix products: 9.73 us -> 0 us
    pallas_call x0 -> x2, Pallas kernels: none -> 36.2 us  [the longest x1 30.2 us: shards(): pl.pallas_call(functools.partial(exchange_kernel, tiles, freqs), out_shap...]
    all_to_all x3 -> x0, starting transfers between devices: 16.9 us -> none  [the longest x1 7.28 us: shards(): lax.all_to_all(w_slots, 'tile', split_axis=0, concat_axis=0, tiled=True)]
    all_to_all x3 -> x0, waiting for transfers between devices: 15.9 us -> none  [the longest x1 10.2 us: shards(): lax.all_to_all(p_slots, 'tile', split_axis=0, concat_axis=0, tiled=True)]
    gather x6 -> x0, local copies, waits for them, and re-layouts: 13.1 us -> none  [the longest x2 6.07 us: pool_from_slots(): return jnp.where(is_live[:, None], flat_slots[source], 0)]
    gather x10 -> x0, other arithmetic: 10.2 us -> none  [the longest x6 10.2 us: pool_owner(): offset = column - begins[owner_tile]]
    dot_general x9 -> x0, matrix products: 9.73 us -> none  [the longest x1 4.89 us: shards(): jnp.einsum('fncs,fct->nst', spectra, time_basis, precision=lax.Precision....]
    convert_element_type x2 -> x0, local copies, waits for them, and re-layouts: 5.69 us -> none  [the longest x1 4.71 us: shards(): return jnp.where(unmuted, signal, 0.0).astype(jnp.bfloat16)]
    unnamed x15 -> x10, local copies, waits for them, and re-layouts: 1.13 us -> 5.27 us
  transfers between devices with their start and end apart: 3 -> 0, of which waited for: 2 -> 0; matrix products, arithmetic and copies ran while one was open for 19% -> 0% of each run, Pallas kernels for 0% -> 0%
where the time goes in v1:
time: 41.7 us; the launch traced here: 41.5 us
  Pallas kernels  36.2 us (87%)
  local copies, waits for them, and re-layouts  5.27 us (13%)
    pallas_call x1, Pallas kernels, shards(): pl.pallas_call(functools.partial(exchange_kernel, tiles, freqs), out_shap...  30.2 us
    pallas_call x1, Pallas kernels, shards(): pl.pallas_call(functools.partial(time_kernel, share, freqs), out_shape=ja...  5.98 us
    unnamed x10, local copies, waits for them, and re-layouts  5.27 us

profile of v1, /device:TPU:0, one launch (start us, length us, event | category | flops | bytes accessed | tf_op | source)
XLA Modules:
  0.0 41.5 jit_solution(12105097301534701151)
XLA Ops:
  0.0 0.0 copy-start.3
  0.0 2.7 %copy.10 = bf16[1,2,512,704]{3,2,1,0:T(8,128)(2,1)} copy(bf16[1,2,512,704]{2,3,1,0:T(8,128)(2,1)} %param.11) | data formatting | bytes 2883584 | tf_op args[2]
  2.7 0.0 copy-done.3
  2.7 1.6 %copy.11 = bf16[1,2,512,704]{3,2,1,0:T(8,128)(2,1)} copy(bf16[1,2,512,704]{2,3,1,0:T(8,128)(2,1)S(1)} %copy-done.3) | data formatting | bytes 2883584 | tf_op args[4]
  4.2 0.0 copy-start.1
  4.2 0.0 copy-start.2
  4.2 30.2 %exchange.1.spec = f32[512,256]{1,0:T(8,128)} custom-call(s32[8,8]{1,0:T(8,128)} %bitcast.11, bf16[512,256]{1,0:T(8,128)(2,1)} %bitcast.9, bf16[512,256]{1,0:T(8,128)(2,1)} %bitcast.10, bf16[2,512,704]{2,1,0:T(8,128)(2,1)} %bitcast.7, f32[1,704]{1,0:T(1,128)} %bitcast.12, bf16[2,512,704]{2,1,0:T(8,128)(2,1)} %bitcast.8, f32[1,704]{1,0:T(1,128)} %bitcast.13), custom_call_target="tpu_custom_call" | custom-call | flops 1476395008 | bytes 2883584 | tf_op jit(solution)/shard_map/exchange/pallas_call | solution.py:341
  34.5 0.0 copy-done.1
  34.5 0.0 copy-done.2
  34.5 0.0 copy-start
  34.5 1.0 %copy-done = f32[512,256]{1,0:T(8,128)S(1)} copy-done((f32[512,256]{1,0:T(8,128)S(1)}, f32[512,256]{1,0:T(8,128)}, u32[]{:S(2)}) %copy-start) | copy-done | bytes 524312
  35.6 6.0 %to_time.1 = bf16[512,32,128]{2,1,0:T(8,128)(2,1)} custom-call(s32[512]{0:T(512)S(1)} %copy-done.2, f32[512,256]{1,0:T(8,128)S(1)} %copy-done, bf16[256,256]{1,0:T(8,128)(2,1)S(1)} %copy-done.1), custom_call_target="tpu_custom_call" | custom-call | tf_op jit(solution)/shard_map/to_time/pallas_call | solution.py:379
Async XLA Ops:
  0.0 2.7 %copy-start.3 = (bf16[1,2,512,704]{2,3,1,0:T(8,128)(2,1)S(1)}, bf16[1,2,512,704]{2,3,1,0:T(8,128)(2,1)}, u32[]{:S(2)}) copy-start(bf16[1,2,512,704]{2,3,1,0:T(8,128)(2,1)} %param.13) | copy-start | bytes 4325380
  4.2 30.3 %copy-start.1 = (bf16[256,256]{1,0:T(8,128)(2,1)S(1)}, bf16[256,256]{1,0:T(8,128)(2,1)}, u32[]{:S(2)}) copy-start(bf16[256,256]{1,0:T(8,128)(2,1)} %constant.2.clone.basis) | copy-start | bytes 393220
  4.2 30.3 %copy-start.2 = (s32[512]{0:T(512)S(1)}, s32[512]{0:T(512)}, u32[]{:S(2)}) copy-start(s32[512]{0:T(512)} %mute.1) | copy-start | bytes 6148
  34.5 1.0 %copy-start = (f32[512,256]{1,0:T(8,128)S(1)}, f32[512,256]{1,0:T(8,128)}, u32[]{:S(2)}) copy-start(f32[512,256]{1,0:T(8,128)} %exchange.1.spec) | copy-start | bytes 1572868

commit v2 on v1

--- a/solution.py
+++ b/solution.py
@@ -41,7 +41,8 @@
     ufac,
     vfac,
     sel,
-    wt,
+    wpool,
+    eye,
     uslot,
     uslot_t,
     vslot,
@@ -62,7 +63,7 @@
     freq = lax.axis_index("freq")
     rows, cols = model.shape
     lanes = cols // HALVES
-    cap = ufac.shape[2]
+    cap = ufac.shape[1]
     slot = cap // tiles
     pad = pool.shape[0] // tiles
     group = sel.shape[0] // pad
@@ -122,37 +123,39 @@
     perm = block_perm()
     pool[...] = jnp.zeros_like(pool)
     loads[0].wait()
-    mt = dot_nt(perm, model[...]).astype(BF)
-
-    step = rows // 4
+    m = dot_nt(model[...], perm).astype(BF)
+
+    step = 2 * slot
 
     def unpack(fac, scale):
-        s = scale[...]
+        diff = lax.broadcasted_iota(jnp.int32, (step, cap), 1) - lax.broadcasted_iota(jnp.int32, (step, cap), 0)
 
         def body(r, carry):
+            s = jnp.sum(jnp.where(diff == r * step, scale[...], 0.0), 1, keepdims=True)
             for c in range(2):
                 at = pl.ds(pl.multiple_of(r * step, step), step)
                 fac[c, at, :] = (fac[c, at, :].astype(F32) * s).astype(BF)
             return carry
 
-        lax.fori_loop(0, rows // step, body, 0)
+        lax.fori_loop(0, cap // step, body, 0)
 
     loads[1].wait()
     unpack(vfac, vscale)
-    a = dot_nn(mt, vfac[0])
-    b = dot_nn(mt, vfac[1])
     hl = lanes // 2
+    lane = lax.broadcasted_iota(jnp.int32, (1, lanes), 1)
+    sign = jnp.where(lane < hl, 1.0, -1.0).astype(F32)
+    a = dot_nn(vfac[0], m)
+    b = dot_nn(vfac[1], m)
     for h in range(HALVES):
-        o = h * lanes
-        wt[o : o + hl, :] = (a[o : o + hl] + b[o + hl : o + lanes]).astype(BF)
-        wt[o + hl : o + lanes, :] = (a[o + hl : o + lanes] - b[o : o + hl]).astype(BF)
+        at = slice(h * lanes, (h + 1) * lanes)
+        wpool[:, at] = (a[:, at] + sign * pltpu.roll(b[:, at], hl, 1)).astype(BF)
     for g in range(groups):
         if groups > 1:
             build_sel(g)
+        w = dot_nn(sel[...], wpool[...]).astype(BF)
         for h in range(HALVES):
-            w = dot_nt(sel[...], wt[h * lanes : (h + 1) * lanes, :]).astype(BF)
             for k in range(group):
-                sbuf[0, h, g * group + k] = w[k * pad : k * pad + slot]
+                sbuf[0, h, g * group + k] = w[k * pad : k * pad + slot, h * lanes : (h + 1) * lanes]
 
     pl.semaphore_wait(barrier, tiles - 1 + freqs - 1)
 
@@ -192,11 +195,8 @@
     send_blocks(0, 0)
     send_blocks(0, 1)
 
-    lane = lax.broadcasted_iota(jnp.int32, (1, lanes), 1)
-    sign = jnp.where(lane < hl, 1.0, -1.0).astype(F32)
-
-    half_rows = rows // 2
-    slots = pool.shape[0]
+    diag = lax.broadcasted_iota(jnp.int32, (rows, rows), 0) == lax.broadcasted_iota(jnp.int32, (rows, rows), 1)
+    eye[...] = jnp.where(diag, 1.0, 0.0).astype(BF)
     srows = group * pad
 
     def to_slots(fac, slots_ref, slots_t_ref):
@@ -204,13 +204,12 @@
             if groups > 1:
                 build_sel(g)
 
-            for r in range(2):
-                at = slice(r * half_rows, (r + 1) * half_rows)
-                for c in range(2):
-                    x = fac[c, at, :]
-                    slots_ref[c, at, g * srows : (g + 1) * srows] = dot_nt(x, sel[...]).astype(BF)
-                    if slots_t_ref is not None:
-                        slots_t_ref[c, g * srows : (g + 1) * srows, at] = dot_nt(sel[...], x).astype(BF)
+            at = slice(g * srows, (g + 1) * srows)
+            for c in range(2):
+                turned = dot_nn(sel[...], fac[c]).astype(BF)
+                if slots_t_ref is not None:
+                    slots_t_ref[c, at, :] = turned
+                slots_ref[c, :, at] = dot_nt(eye[...], turned).astype(BF)
 
     loads[2].wait()
     unpack(ufac, uscale)
@@ -277,7 +276,7 @@
             share_copy(h, d, True).wait_recv()
         parts = swap_groups([frecv[h, f].astype(F32) for f in range(freqs)])
         for g in range(freqs):
-            out[g * brows : (g + 1) * brows, h * lanes : (h + 1) * lanes] = parts[g]
+            out[g * brows : (g + 1) * brows, h * lanes : (h + 1) * lanes] = parts[g].astype(BF)
 
     for h in range(HALVES):
         for phase in range(2):
@@ -293,41 +292,48 @@
     start = pl.program_id(0) * block
     half = depth // HALVES
     part = share // HALVES
-    s = lax.broadcasted_iota(jnp.int32, (share, depth), 0)
-    k = lax.broadcasted_iota(jnp.int32, (share, depth), 1)
-    keep = (k // half == s // part) & (k % part == s % part)
-    mask = jnp.where(keep, 1.0, 0.0).astype(BF)
+    s = lax.broadcasted_iota(jnp.int32, (part, half), 0)
+    k = lax.broadcasted_iota(jnp.int32, (part, half), 1)
+    keep = k % part == s
     table = basis[...]
-    t = lax.broadcasted_iota(jnp.int32, (share, NTIME), 1)
-    batch = 8
+    t = lax.broadcasted_iota(jnp.int32, (part, NTIME), 1)
+    batch = 16
     for n0 in range(0, block, batch):
+        g = spec[n0 : n0 + batch, :].astype(F32)
         rows = []
-        for n in range(n0, n0 + batch):
-            row = jnp.broadcast_to(spec[n : n + 1, :], (share, depth)).astype(BF)
-            rows.append(row * mask)
-        both = dot_nn(jnp.concatenate(rows, 0), table)
-        signal = both[:, :NTIME] + both[:, NTIME:]
-        for n in range(n0, n0 + batch):
-            o = (n - n0) * share
-            live = t >= mute[start + n]
-            out[n] = jnp.where(live, signal[o : o + share], 0.0).astype(BF)
+        for n in range(0, batch, 2):
+            for h in range(HALVES):
+                at = slice(h * half, (h + 1) * half)
+                pair = [
+                    jnp.where(keep, jnp.broadcast_to(g[n + e : n + e + 1, at], (part, half)), 0.0).astype(BF)
+                    for e in range(2)
+                ]
+                rows.append(jnp.concatenate(pair, 1))
+        signal = dot_nn(jnp.concatenate(rows, 0), table)
+        for n in range(batch):
+            live = t >= mute[start + n0 + n]
+            e = n % 2
+            for h in range(HALVES):
+                o = ((n // 2) * HALVES + h) * part
+                piece = signal[o : o + part, e * NTIME : (e + 1) * NTIME]
+                out[n0 + n, h * part : (h + 1) * part, :] = jnp.where(live, piece, 0.0).astype(BF)
 
 
 def time_table(freqs, share):
     part = share // HALVES
-    k = np.arange(2 * share * freqs)
+    k = np.arange(share * freqs)
     f = (k % (part * freqs)) // part
-    c = (k % (2 * part * freqs)) // (part * freqs)
+    c = k // (part * freqs)
     angle = 2.0 * math.pi * (f[:, None] + 1) * np.arange(NTIME)[None, :] / NTIME
     table = 0.5 * np.where(c[:, None] == 0, np.cos(angle), -np.sin(angle))
-    high = table.astype(jnp.bfloat16)
-    low = (table - high.astype(np.float64)).astype(jnp.bfloat16)
-    return np.concatenate([high, low], 1)
+    return np.kron(np.eye(2), table).astype(jnp.bfloat16)
 
 
 def shards(tiles, freqs, model_field, data_field, u_codes, u_scales, v_codes, v_scales, tile_ranks, mute_start):
     rows, cols = model_field.shape[1:]
     cap = u_codes.shape[3]
+    u_turned = jnp.swapaxes(u_codes[0], 1, 2)
+    v_turned = jnp.swapaxes(v_codes[0], 1, 2)
     slot = cap // tiles
     pad = -(-slot // 32) * 32
     slots = tiles * pad
@@ -340,16 +346,17 @@
     smem = pl.BlockSpec(memory_space=pltpu.SMEM)
     spectra = pl.pallas_call(
         functools.partial(exchange_kernel, tiles, freqs),
-        out_shape=jax.ShapeDtypeStruct((rows, cols), F32),
+        out_shape=jax.ShapeDtypeStruct((rows, cols), BF),
         in_specs=[smem, any_spec, any_spec, any_spec, vmem, any_spec, vmem],
         out_specs=vmem,
         scratch_shapes=[
             pltpu.VMEM((rows, cols), BF),
             pltpu.VMEM((rows, cols), BF),
-            pltpu.VMEM((2, rows, cap), BF),
-            pltpu.VMEM((2, rows, cap), BF),
+            pltpu.VMEM((2, cap, rows), BF),
+            pltpu.VMEM((2, cap, rows), BF),
             pltpu.VMEM((group * pad, cap), BF),
-            pltpu.VMEM((cols, cap), BF),
+            pltpu.VMEM((cap, cols), BF),
+            pltpu.VMEM((rows, rows), BF),
             pltpu.VMEM((2, rows, slots), BF),
             pltpu.VMEM((2, slots, rows), BF),
             pltpu.VMEM((2, rows, slots), BF),
@@ -373,7 +380,7 @@
             flops=16 * rows * cap * cols, bytes_accessed=8 * rows * cap, transcendentals=0
         ),
         name="exchange",
-    )(tile_ranks[0], model_field[0], data_field[0], u_codes[0], u_scales[0], v_codes[0], v_scales[0])
+    )(tile_ranks[0], model_field[0], data_field[0], u_turned, u_scales[0], v_turned, v_scales[0])
     table = jnp.asarray(time_table(freqs, share))
     block = 64
     return pl.pallas_call(

time: 41.7 us -> 37.2 us (0.89)
  local copies, waits for them, and re-layouts: 5.27 us -> 0.95 us
    unnamed x10 -> x6, local copies, waits for them, and re-layouts: 5.27 us -> 0.95 us
    pallas_call x1, Pallas kernels: 5.98 us -> 5.3 us  [shards(): pl.pallas_call(functools.partial(time_kernel, share, freqs), out_shape=ja...]
    pallas_call x1, Pallas kernels: 30.2 us -> 30.7 us  [shards(): pl.pallas_call(functools.partial(exchange_kernel, tiles, freqs), out_shap...]
where the time goes in v2:
time: 37.2 us; the launch traced here: 37 us
  Pallas kernels  36 us (97%)
  local copies, waits for them, and re-layouts  0.95 us (3%)
    pallas_call x1, Pallas kernels, shards(): pl.pallas_call(functools.partial(exchange_kernel, tiles, freqs), out_shap...  30.7 us
    pallas_call x1, Pallas kernels, shards(): pl.pallas_call(functools.partial(time_kernel, share, freqs), out_shape=ja...  5.3 us
    unnamed x6, local copies, waits for them, and re-layouts  0.95 us

profile of v2, /device:TPU:0, one launch (start us, length us, event | category | flops | bytes accessed | tf_op | source)
XLA Modules:
  0.0 37.0 jit_solution(51686768387937051)
XLA Ops:
  0.0 0.0 copy-start.1
  0.0 0.0 copy-start.2
  0.0 30.7 %exchange.1.spec = bf16[512,256]{1,0:T(8,128)(2,1)} custom-call(s32[8,8]{1,0:T(8,128)} %bitcast.15, bf16[512,256]{1,0:T(8,128)(2,1)} %bitcast.13, bf16[512,256]{1,0:T(8,128)(2,1)} %bitcast.14, bf16[2,704,512]{2,1,0:T(8,128)(2,1)} %bitcast.11, f32[1,704]{1,0:T(1,128)} %bitcast.16, bf16[2,704,512]{2,1,0:T(8,128)(2,1)} %bitcast.12, f32[1,704]{1,0:T(1,128)} %bitcast.17), custom_call_target="tpu_custom_call" | custom-call | flops 1476395008 | bytes 2883584 | tf_op jit(solution)/shard_map/exchange/pallas_call | solution.py:347
  30.7 0.0 copy-done.1
  30.7 0.0 copy-done.2
  30.7 0.0 copy-start
  30.8 0.9 %copy-done = bf16[512,256]{1,0:T(8,128)(2,1)S(1)} copy-done((bf16[512,256]{1,0:T(8,128)(2,1)S(1)}, bf16[512,256]{1,0:T(8,128)(2,1)}, u32[]{:S(2)}) %copy-start) | copy-done | bytes 262168
  31.7 5.3 %to_time.1 = bf16[512,32,128]{2,1,0:T(8,128)(2,1)} custom-call(s32[512]{0:T(512)S(1)} %copy-done.2, bf16[512,256]{1,0:T(8,128)(2,1)S(1)} %copy-done, bf16[256,256]{1,0:T(8,128)(2,1)S(1)} %copy-done.1), custom_call_target="tpu_custom_call" | custom-call | tf_op jit(solution)/shard_map/to_time/pallas_call | solution.py:386
Async XLA Ops:
  0.0 30.7 %copy-start.1 = (bf16[256,256]{1,0:T(8,128)(2,1)S(1)}, bf16[256,256]{1,0:T(8,128)(2,1)}, u32[]{:S(2)}) copy-start(bf16[256,256]{1,0:T(8,128)(2,1)} %constant.2.clone.basis) | copy-start | bytes 393220
  0.0 30.7 %copy-start.2 = (s32[512]{0:T(512)S(1)}, s32[512]{0:T(512)}, u32[]{:S(2)}) copy-start(s32[512]{0:T(512)} %mute.1) | copy-start | bytes 6148
  30.7 1.0 %copy-start = (bf16[512,256]{1,0:T(8,128)(2,1)S(1)}, bf16[512,256]{1,0:T(8,128)(2,1)}, u32[]{:S(2)}) copy-start(bf16[512,256]{1,0:T(8,128)(2,1)} %exchange.1.spec) | copy-start | bytes 786436

commit v3 on v2

--- a/solution.py
+++ b/solution.py
@@ -231,8 +231,7 @@
         for i in range(tiles):
             sbuf[1, h, i] = p[i * pad : i * pad + slot]
         send_blocks(1, h)
-        if h == 0:
-            to_slots(vfac, vslot, None)
+    to_slots(vfac, vslot, None)
 
     def swap_groups(pieces):
         out_pieces = []
@@ -297,7 +296,7 @@
     keep = k % part == s
     table = basis[...]
     t = lax.broadcasted_iota(jnp.int32, (part, NTIME), 1)
-    batch = 16
+    batch = block
     for n0 in range(0, block, batch):
         g = spec[n0 : n0 + batch, :].astype(F32)
         rows = []

time: 37.2 us -> 36.5 us (0.981)
  Pallas kernels: 36 us -> 35.4 us
    pallas_call x1, Pallas kernels: 30.7 us -> 30.1 us  [shards(): pl.pallas_call(functools.partial(exchange_kernel, tiles, freqs), out_shap...]
where the time goes in v3:
time: 36.5 us; the launch traced here: 36.4 us
  Pallas kernels  35.4 us (97%)
  local copies, waits for them, and re-layouts  0.95 us (3%)
    pallas_call x1, Pallas kernels, shards(): pl.pallas_call(functools.partial(exchange_kernel, tiles, freqs), out_shap...  30.1 us
    pallas_call x1, Pallas kernels, shards(): pl.pallas_call(functools.partial(time_kernel, share, freqs), out_shape=ja...  5.25 us
    unnamed x6, local copies, waits for them, and re-layouts  0.95 us

profile of v3, /device:TPU:0, one launch (start us, length us, event | category | flops | bytes accessed | tf_op | source)
XLA Modules:
  0.0 36.4 jit_solution(12751322117957590738)
XLA Ops:
  0.0 0.0 copy-start.1
  0.0 0.0 copy-start.2
  0.0 30.1 %exchange.1.spec = bf16[512,256]{1,0:T(8,128)(2,1)} custom-call(s32[8,8]{1,0:T(8,128)} %bitcast.15, bf16[512,256]{1,0:T(8,128)(2,1)} %bitcast.13, bf16[512,256]{1,0:T(8,128)(2,1)} %bitcast.14, bf16[2,704,512]{2,1,0:T(8,128)(2,1)} %bitcast.11, f32[1,704]{1,0:T(1,128)} %bitcast.16, bf16[2,704,512]{2,1,0:T(8,128)(2,1)} %bitcast.12, f32[1,704]{1,0:T(1,128)} %bitcast.17), custom_call_target="tpu_custom_call" | custom-call | flops 1476395008 | bytes 2883584 | tf_op jit(solution)/shard_map/exchange/pallas_call | solution.py:346
  30.1 0.0 copy-done.1
  30.1 0.0 copy-done.2
  30.2 0.0 copy-start
  30.2 0.9 %copy-done = bf16[512,256]{1,0:T(8,128)(2,1)S(1)} copy-done((bf16[512,256]{1,0:T(8,128)(2,1)S(1)}, bf16[512,256]{1,0:T(8,128)(2,1)}, u32[]{:S(2)}) %copy-start) | copy-done | bytes 262168
  31.1 5.3 %to_time.1 = bf16[512,32,128]{2,1,0:T(8,128)(2,1)} custom-call(s32[512]{0:T(512)S(1)} %copy-done.2, bf16[512,256]{1,0:T(8,128)(2,1)S(1)} %copy-done, bf16[256,256]{1,0:T(8,128)(2,1)S(1)} %copy-done.1), custom_call_target="tpu_custom_call" | custom-call | tf_op jit(solution)/shard_map/to_time/pallas_call | solution.py:385
Async XLA Ops:
  0.0 30.1 %copy-start.1 = (bf16[256,256]{1,0:T(8,128)(2,1)S(1)}, bf16[256,256]{1,0:T(8,128)(2,1)}, u32[]{:S(2)}) copy-start(bf16[256,256]{1,0:T(8,128)(2,1)} %constant.2.clone.basis) | copy-start | bytes 393220
  0.0 30.1 %copy-start.2 = (s32[512]{0:T(512)S(1)}, s32[512]{0:T(512)}, u32[]{:S(2)}) copy-start(s32[512]{0:T(512)} %mute.1) | copy-start | bytes 6148
  30.2 1.0 %copy-start = (bf16[512,256]{1,0:T(8,128)(2,1)S(1)}, bf16[512,256]{1,0:T(8,128)(2,1)}, u32[]{:S(2)}) copy-start(bf16[512,256]{1,0:T(8,128)(2,1)} %exchange.1.spec) | copy-start | bytes 786436
